TPU v7x, 32 devices: a whole 2x2x4 slice. The times are simulated.
32 devices in a mesh: mod: 16 (over z, y, x), pair: 2 (over core).
Axes of the slice: x: 2, y: 2, z: 4, core: 2. Of those that a mesh axis runs over, the one named last changes fastest.
Arguments:
- query_grads: bfloat16 [128, 64, 16, 128], P(('mod', 'pair')), may hold values from -6 to 6
- train_grads: bfloat16 [1024, 64, 16, 128], P('pair', 'mod'), may hold values from -6 to 6
- left_basis: bfloat16 [64, 16, 16], P('mod'), may hold values from -1.5 to 1.5
- right_basis: bfloat16 [64, 128, 128], P('mod'), may hold values from -0.5 to 0.5
- eigenvalues: bfloat16 [64, 16, 128], P('mod'), may hold values from 0.0009994507 to 10
- block_rows: int32 [64], P('mod'), may hold values from 0 to 16, as said below
Outputs:
- scores: float32 [128, 1024], P('mod', 'pair')
Inputs may be any that keep to these rules, and one draw needn't show every extreme that they name: `block_rows`: owner j of the 16 owners holds slots j * 4 to (j + 1) * 4 - 1; of these the first 1 to 4 are live with 8 to 16 rows each and the rest hold 0; some owner has all 4 slots live and a slot of 16 rows, and some live slot has 8 rows.
All inputs are finite; a program needn't handle non-finite values.
Results may differ from a plain program's by a relative error of at most 0.0047.
Values may be sent and summed in bfloat16 or wider, within the bound.
A program may use at most 128 MiB of HBM per device.

v0:
```python
import math

import jax
import jax.numpy as jnp
from jax import lax
from jax.sharding import PartitionSpec as P


def swapped(value, axis, stride):
    mask = 2**stride
    pairs = [(source, source ^ mask) for source in range(lax.axis_size(axis))]
    return lax.ppermute(value, axis, pairs)


def precondition(grad_slot, left_factor, right_factor, eig_block, live_rows):
    count_n, row_total, col_total = grad_slot.shape
    row_mask = (jnp.arange(row_total) < live_rows).astype(jnp.float32)
    left_masked = (left_factor.astype(jnp.float32) * row_mask[:, None] * row_mask[None, :]).astype(
        jnp.bfloat16
    )
    masked_grads = (grad_slot.astype(jnp.float32) * row_mask[None, :, None]).astype(jnp.bfloat16)
    rotated_right = (
        jnp.dot(
            masked_grads.reshape(count_n * row_total, col_total),
            right_factor,
            preferred_element_type=jnp.float32,
        )
        .astype(jnp.bfloat16)
        .reshape(count_n, row_total, col_total)
    )
    rotated = jnp.einsum(
        "ba,nbc->nac", left_masked, rotated_right, preferred_element_type=jnp.float32
    )
    eig_float = eig_block.astype(jnp.float32)
    damping = (
        0.1
        * jnp.sum(eig_float * row_mask[:, None])
        / jnp.maximum(live_rows * col_total, 1).astype(jnp.float32)
    )
    scaled = (rotated / (eig_float + damping)).astype(jnp.bfloat16)
    back_right = (
        jnp.dot(
            scaled.reshape(count_n * row_total, col_total),
            right_factor.T,
            preferred_element_type=jnp.float32,
        )
        .astype(jnp.bfloat16)
        .reshape(count_n, row_total, col_total)
    )
    return jnp.einsum(
        "ab,nbc->nac", left_masked, back_right, preferred_element_type=jnp.float32
    ).astype(jnp.bfloat16)


def precondition_slots(grads, left_all, right_all, eig_all, rows_all):
    slot_count = grads.shape[1]

    def slot_turn(slot_index, output):
        grad_slot = lax.dynamic_index_in_dim(grads, slot_index, 1, keepdims=False)
        live_rows = rows_all[slot_index]
        result = lax.cond(
            live_rows > 0,
            lambda: precondition(
                grad_slot,
                left_all[slot_index],
                right_all[slot_index],
                eig_all[slot_index],
                live_rows,
            ),
            lambda: jnp.zeros(grad_slot.shape, jnp.bfloat16),
        )
        return lax.dynamic_update_index_in_dim(output, result, slot_index, 1)

    return lax.fori_loop(0, slot_count, slot_turn, jnp.zeros(grads.shape, jnp.bfloat16))


def score_block(left_rows, right_rows):
    return lax.dot_general(
        left_rows, right_rows, (((1,), (1,)), ((), ())), preferred_element_type=jnp.float32
    )


def on_device(query_grads, train_grads, left_basis, right_basis, eigenvalues, block_rows):
    slot_total = query_grads.shape[1]
    norm_scale = 1.0 / math.sqrt(slot_total * query_grads.shape[2] * query_grads.shape[3])
    per_source = query_grads.shape[0]
    received = lax.all_to_all(query_grads, "mod", split_axis=1, concat_axis=0, tiled=True)
    result = precondition_slots(received, left_basis, right_basis, eigenvalues, block_rows)
    own_half = result.reshape(result.shape[0], -1)
    train_flat = train_grads.reshape(train_grads.shape[0], -1)
    pair_side = lax.axis_index("pair")
    partner = swapped(own_half, "pair", 0)
    own_scores = score_block(own_half, train_flat)
    far_scores = score_block(partner, train_flat)
    low_half = jnp.where(pair_side == 0, own_scores, far_scores)
    high_half = jnp.where(pair_side == 0, far_scores, own_scores)
    block_count = 2 * per_source * lax.axis_size("mod") // (2 * per_source)
    stacked = jnp.stack(
        [
            low_half.reshape(block_count, per_source, -1),
            high_half.reshape(block_count, per_source, -1),
        ],
        1,
    )
    summed = lax.psum_scatter(
        stacked.reshape(2 * per_source * lax.axis_size("mod"), -1),
        "mod",
        scatter_dimension=0,
        tiled=True,
    )
    return summed * norm_scale


def solution(mesh):
    placed = (
        P(("mod", "pair"), None, None, None),
        P("pair", "mod", None, None),
        P("mod", None, None),
        P("mod", None, None),
        P("mod", None, None),
        P("mod"),
    )
    return jax.shard_map(
        on_device, mesh=mesh, in_specs=placed, out_specs=P("mod", "pair"), check_vma=False
    )
```

profile of v0, /device:TPU:0, one launch (start us, length us, event | category | flops | bytes accessed | tf_op | source)
XLA Modules:
  0.0 191.9 jit_solution(14513497341231982138)
XLA Ops:
  6.5 2.5 %copy.19 = bf16[4,64,16,128]{3,2,0,1:T(8,128)(2,1)} copy(bf16[4,64,16,128]{3,2,1,0:T(8,128)(2,1)} %param.10) | data formatting | bytes 2097152 | tf_op args[0]
  9.0 8.3 %all-to-all-start = ((bf16[4,64,16,128]{3,2,0,1:T(8,128)(2,1)}), bf16[4,64,16,128]{3,2,0,1:T(8,128)(2,1)S(1)}, u32[]{:S(2)}, u32[]{:S(2)}) async-start(bf16[4,64,16,128]{3,2,0,1:T(8,128)(2,1)} %copy.19), calls=%async_computation | async-start | bytes 2097152 | tf_op jit(solution)/shard_map/all_to_all | solution.py:87
  17.4 0.0 reduce-scatter.2.cloned.1.call-start
  17.4 24.4 %all-to-all-done = bf16[4,64,16,128]{3,2,0,1:T(8,128)(2,1)S(1)} async-done(((bf16[4,64,16,128]{3,2,0,1:T(8,128)(2,1)}), bf16[4,64,16,128]{3,2,0,1:T(8,128)(2,1)S(1)}, u32[]{:S(2)}, u32[]{:S(2)}) %all-to-all-start) | async-done | bytes 1048608 | tf_op jit(solution)/shard_map/all_to_all | solution.py:87
  41.8 0.3 copy.20
  42.1 16.2 %while.13 = (s32[]{:T(128)}, bf16[64,4,16,128]{3,2,0,1:T(8,128)(2,1)S(1)}, s32[4]{0:T(128)}, bf16[64,4,16,128]{3,2,1,0:T(8,128)(2,1)S(1)}, bf16[4,128,128]{2,1,0...) while((s32[]{:T(128)}, ...), condition=%wide.region_4.5_spmd, body=%wide.region_0.4_spmd.sunk | while | flops 76558368 | bytes 3246581 | solution.py:74
  42.1 1.3 dynamic_slice.45
  44.0 8.3 %conditional.2 = (bf16[64,1,16,128]{3,2,0,1:T(8,128)(2,1)S(1)}) conditional(s32[]{:T(128)} %convert_element_type.116, () %tuple.41, (bf16[64,4,16,128]{3,2,1,0:T(8,128)(2,1)S(1)}, s32[]{:T(128)}, s32[]{:T(128)}, bf16[4,128,128]{2,1,0:T(8,128)(2,1)}, bf16[4,16,16]{2,1,0:T(8,128)(2,1)}, /*index=5*/bf16[4,16,128]{2,1,0:T(8,128)(2,1)}) %tuple.42), branch_computations={%region_1.1_spmd, %region_2.3_spmd} | conditional | flops 76558368 | bytes 2722122 | solution.py:61
  44.0 0.6 compare_convert_fusion
  44.6 1.4 fusion.9
  47.4 0.7 fusion.7
  48.1 0.1 multiply_convert_fusion
  48.3 1.0 convolution_convert_fusion.2
  49.2 1.0 fusion.1
  50.3 1.0 convolution_convert_fusion.1
  51.3 1.0 fusion.2
  52.3 1.3 dynamic_slice.45
  54.2 0.1 conditional.2
  54.3 1.3 dynamic_slice.45
  56.2 0.1 conditional.2
  56.3 1.3 dynamic_slice.45
  58.2 0.1 conditional.2
  58.3 0.3 copy.23
  58.6 0.7 copy.43
  59.3 0.1 collective-permute-start
  59.4 11.7 %fusion.20 = f32[64,512]{1,0:T(8,128)S(1)} fusion(bf16[512,4,16,128]{3,2,1,0:T(8,128)(2,1)} %param.11, bf16[64,4,16,128]{3,2,0,1:T(8,128)(2,1)S(1)} %get-tuple-element.173), kind=kOutput, calls=%fused_computation.28 | convolution fusion | flops 536870912 | bytes 9568256 | tf_op jit(solution)/shard_map/dot_general | solution.py:78
  71.2 11.9 %broadcast_select_fusion.1 = (f32[64,512]{1,0:T(8,128)S(1)}, f32[64,512]{1,0:T(8,128)S(1)}) fusion(f32[64,512]{1,0:T(8,128)S(1)} %fusion.20, pred[]{:T(512)S(6)} %eq.4, bf16[64,8192]{1,0:T(8,128)(2,1)S(1)} %collective-permute-done, bf16[64,8,64,128]{3,2,1,0:T(8,128)(2,1)} %bitcast.70), kind=kOutput, calls=%fused_computation.33 | convolution fusion | flops 536936448 | bytes 9830401 | tf_op jit(solution)/shard_map/dot_general | solution.py:78
  83.2 0.1 pad_maximum_fusion
  83.3 0.8 reshape.79
  84.1 0.0 reduce-scatter.2.cloned.1.call-update
  84.1 99.6 %reduce-scatter.2.cloned.1.call-done = f32[8,512]{1,0:T(8,128)} async-done(((f32[128,512]{1,0:T(8,128)}), f32[8,512]{1,0:T(8,128)}) %reduce-scatter.2.cloned.1.call-update) | async-done | bytes 16400 | tf_op jit(solution)/shard_map/reduce_scatter | solution.py:105
  183.7 1.3 broadcast_multiply_fusion
  (12 shorter events, 0.4 us)
Async XLA Ops:
  9.0 32.8 %all-to-all-start = ((bf16[4,64,16,128]{3,2,0,1:T(8,128)(2,1)}), bf16[4,64,16,128]{3,2,0,1:T(8,128)(2,1)S(1)}, u32[]{:S(2)}, u32[]{:S(2)}) async-start(bf16[4,64,16,128]{3,2,0,1:T(8,128)(2,1)} %copy.19), calls=%async_computation | async-start | bytes 2097152 | tf_op jit(solution)/shard_map/all_to_all | solution.py:87
  17.4 166.3 %reduce-scatter.2.cloned.1.call-start = ((), (), s32[]{:S(2)}) async-start(), calls=%async_computation.2 | async-start | bytes 278528 | tf_op jit(solution)/shard_map/reduce_scatter | solution.py:105
  59.3 11.8 %collective-permute-start = (bf16[64,8192]{1,0:T(8,128)(2,1)S(1)}, bf16[64,8192]{1,0:T(8,128)(2,1)S(1)}, u32[]{:S(2)}, u32[]{:S(2)}) collective-permute-start(bf16[64,8192]{1,0:T(8,128)(2,1)S(1)} %bitcast.69), channel_id=1, source_target_pairs={{0,1},{1,0},{2,3},{3,2},{4,5},{5,4},{6,7},{7,6},{8,9},{9,8},{10,11... | collective-permute-start | bytes 3145736 | tf_op jit(solution)/shard_map/ppermute | solution.py:12
Sparse Core Ops, SparseCore 0:
  84.2 99.4 reduce-scatter.1
where the time goes:
time: 194 us; the launch traced here: 192 us
  waiting for transfers between devices  124 us (64%)
  matrix products  27.6 us (14%)
  between operations  13.5 us (7%)
  local copies, waits for them, and re-layouts  9.95 us (5%)
  starting transfers between devices  8.42 us (4%)
  other arithmetic  4.27 us (2%)
  loops' own time  4.1 us (2%)
    reduce_scatter x1, waiting for transfers between devices, on_device(): lax.psum_scatter(stacked.reshape(2 * per_source * lax.axis_size('mod'), -...  99.6 us
    all_to_all x1, waiting for transfers between devices, on_device(): lax.all_to_all(query_grads, 'mod', split_axis=1, concat_axis=0, tiled=True)  24.4 us
    dot_general x2, matrix products, score_block(): lax.dot_general(left_rows, right_rows, (((1,), (1,)), ((), ())), preferre...  23.7 us
    all_to_all x1, starting transfers between devices, on_device(): lax.all_to_all(query_grads, 'mod', split_axis=1, concat_axis=0, tiled=True)  8.31 us
    dynamic_slice x4, local copies, waits for them, and re-layouts, slot_turn(): live_rows = rows_all[slot_index]  5 us
  transfers between devices with their start and end apart: 3, of which 2 were waited for; matrix products, arithmetic and copies ran while one was open for 6% of the time, Pallas kernels for 0%

commit v1 on v0

v1 whole, which is shorter than its diff:
```python
import functools
import math

import jax
import jax.numpy as jnp
from jax import lax
from jax.experimental import pallas as pl
from jax.experimental.pallas import tpu as pltpu
from jax.sharding import PartitionSpec as P

MESH = pl.DeviceIdType.MESH
GROUP = 16
F32 = jnp.float32
BF16 = jnp.bfloat16


def iota(shape, dim):
    return lax.broadcasted_iota(jnp.int32, shape, dim)


def dot(a, b):
    return jnp.dot(a, b, preferred_element_type=F32)


def dot_t(a, b):
    return lax.dot_general(a, b, (((1,), (1,)), ((), ())), preferred_element_type=F32)


def turn(rows, right, mixer):
    half = rows.shape[0] // 2
    rotated_right = dot(rows, right).astype(BF16)
    side = jnp.concatenate([rotated_right[:half], rotated_right[half:]], axis=1)
    return dot(mixer, side)


def kernel(
    n,
    q_ref, t_ref, left_ref, right_ref, eig_ref, rows_ref,
    out_ref,
    recv, tv, tr, sc, mixer, recip, acc, perm, msg, got,
    send_sem, recv_sem, t_sem, pair_send, pair_recv, msg_send, msg_recv,
):
    per, _, rows, cols = q_ref.shape
    trains, slots = t_ref.shape[0], t_ref.shape[1]
    queries = n * per
    me = lax.axis_index("mod")
    side = lax.axis_index("pair")
    other = 1 - side

    def peer(i):
        return lax.rem(me + 1 + lax.rem(n // 2 - 1 + i, n - 1), n)

    barrier = pltpu.get_barrier_semaphore()

    def greet(i, carry):
        pl.semaphore_signal(barrier, inc=1, device_id=(peer(i), side), device_id_type=MESH)
        return carry

    lax.fori_loop(0, n - 1, greet, 0)
    pl.semaphore_signal(barrier, inc=1, device_id=(me, other), device_id_type=MESH)

    parts = t_sem.shape[0]
    part = trains // parts

    def train_copy(i):
        return pltpu.make_async_copy(
            t_ref.at[pl.ds(i * part, part)], tv.at[pl.ds(i * part, part)], t_sem.at[i]
        )

    for i in range(parts):
        train_copy(i).start()

    pl.semaphore_wait(barrier, n)

    for k in range(slots):
        def send(i, carry, k=k):
            to = peer(i)
            pltpu.make_async_remote_copy(
                src_ref=q_ref.at[:, to * slots + k],
                dst_ref=recv.at[k, pl.ds(me * per, per)],
                send_sem=send_sem,
                recv_sem=recv_sem.at[k],
                device_id=(to, side),
                device_id_type=MESH,
            ).start()
            return carry

        lax.fori_loop(0, n - 1, send, 0)
        pltpu.make_async_copy(
            q_ref.at[:, me * slots + k], recv.at[k, pl.ds(me * per, per)], recv_sem.at[k]
        ).start()

    big = GROUP * rows
    pick_a = (iota((big, rows), 0) // GROUP == iota((big, rows), 1)).astype(BF16)
    pick_b = (lax.rem(iota((rows, big), 1), rows) == iota((rows, big), 0)).astype(BF16)
    same = lax.rem(iota((big, big), 0), GROUP) == iota((big, big), 1) // rows
    for s in range(slots):
        live = rows_ref[s]
        keep = (iota((rows, rows), 0) < live) & (iota((rows, rows), 1) < live)
        left = jnp.where(keep, left_ref[s].astype(F32), 0.0).astype(BF16)
        spread = dot(dot_t(pick_a, left).astype(BF16), pick_b)
        mixer[s] = jnp.where(same, spread, 0.0).astype(BF16)
        eig = eig_ref[s].astype(F32)
        kept = jnp.where(iota((rows, cols), 0) < live, eig, 0.0)
        width = jnp.maximum(live * cols, 1).astype(F32)
        damping = 0.1 * jnp.sum(jnp.sum(kept, axis=1, keepdims=True), axis=0, keepdims=True) / width
        inverse = 1.0 / (eig + damping)
        for a in range(rows):
            block = jnp.broadcast_to(inverse[a : a + 1], (GROUP, cols))
            recip[s, a * GROUP : (a + 1) * GROUP] = jnp.concatenate([block, block], axis=1)

    wide = trains // 2
    total = perm.shape[0]
    out_row = iota((total, total), 0)
    in_row = iota((total, total), 1)
    owner = out_row // (4 * per)
    column_half = lax.rem(out_row // (2 * per), 2)
    far = lax.rem(lax.rem(out_row // per, 2) + side, 2)
    want = ((column_half * 2 + far) * n + owner) * per + lax.rem(out_row, per)
    perm[...] = (in_row == want).astype(BF16)

    def rotate_train(step, carry):
        base = step * 2 * GROUP
        for s in range(slots):
            block = tv[pl.ds(base, 2 * GROUP), s].reshape(2 * big, cols)
            turned = turn(block, right_ref[s], mixer[s]).astype(BF16)
            for half in range(2):
                for a in range(rows):
                    tr[s, pl.ds(pl.multiple_of(base + half * GROUP, GROUP), GROUP), a * cols : (a + 1) * cols] = turned[
                        a * GROUP : (a + 1) * GROUP, half * cols : (half + 1) * cols
                    ]
        return carry

    for i in range(parts):
        train_copy(i).wait()
        steps = part // (2 * GROUP)
        lax.fori_loop(i * steps, (i + 1) * steps, rotate_train, 0)

    def exchange(k):
        return pltpu.make_async_remote_copy(
            src_ref=sc.at[k, 0],
            dst_ref=sc.at[k, 1],
            send_sem=pair_send.at[k],
            recv_sem=pair_recv.at[k],
            device_id=(me, other),
            device_id_type=MESH,
        )

    acc[...] = jnp.zeros_like(acc)
    for k in range(slots):
        pltpu.make_async_copy(recv.at[k], recv.at[k], recv_sem.at[k]).wait()
        mask = (iota((rows, cols), 0) < rows_ref[k]).astype(F32).astype(BF16)
        for g in range(queries // (2 * GROUP)):
            base = g * 2 * GROUP
            block = (recv[k, base : base + 2 * GROUP] * mask[None]).reshape(2 * big, cols)
            scaled = (turn(block, right_ref[k], mixer[k]) * recip[k]).astype(BF16)
            for half in range(2):
                for a in range(rows):
                    sc[k, 0, base + half * GROUP : base + (half + 1) * GROUP, a * cols : (a + 1) * cols] = scaled[
                        a * GROUP : (a + 1) * GROUP, half * cols : (half + 1) * cols
                    ]
        exchange(k).start()
        if k > 0:
            exchange(k - 1).wait()
            both = sc[k - 1].reshape(2 * queries, rows * cols)
            acc[...] += dot_t(both, tr[k - 1])
    last = slots - 1
    acc[:queries] += dot_t(sc[last, 0], tr[last])
    exchange(last).wait()
    acc[queries:] += dot_t(sc[last, 1], tr[last])

    stacked = jnp.concatenate([acc[:, :wide], acc[:, wide:]], axis=0).astype(BF16)
    msg[...] = dot(perm[...], stacked).astype(BF16).reshape(msg.shape)

    def post(i, carry):
        to = peer(i)
        pltpu.make_async_remote_copy(
            src_ref=msg.at[to],
            dst_ref=got.at[me],
            send_sem=msg_send,
            recv_sem=msg_recv,
            device_id=(to, side),
            device_id_type=MESH,
        ).start()
        return carry

    lax.fori_loop(0, n - 1, post, 0)
    pltpu.make_async_copy(msg.at[me], got.at[me], msg_recv).start()
    sent = q_ref.at[:, pl.ds(0, (n - 1) * slots)]
    pltpu.make_async_copy(sent, sent, send_sem).wait()
    pltpu.make_async_copy(got, got, msg_recv).wait()
    summed = jnp.sum(got[...].astype(F32), axis=0)
    out_ref[:, :wide] = summed[: 2 * per]
    out_ref[:, wide:] = summed[2 * per :]
    posted = msg.at[pl.ds(0, n - 1)]
    pltpu.make_async_copy(posted, posted, msg_send).wait()


def on_device(n, query_grads, train_grads, left_basis, right_basis, eigenvalues, block_rows):
    per, slot_total, rows, cols = query_grads.shape
    trains, slots = train_grads.shape[:2]
    queries = n * per
    big = GROUP * rows
    wide = trains // 2
    norm_scale = 1.0 / math.sqrt(slot_total * rows * cols)
    vmem = pl.BlockSpec(memory_space=pltpu.VMEM)
    parts = pl.BlockSpec(memory_space=pl.ANY)
    dma = pltpu.SemaphoreType.DMA
    scores = pl.pallas_call(
        functools.partial(kernel, n),
        out_shape=jax.ShapeDtypeStruct((2 * per, trains), F32),
        in_specs=[parts, parts, vmem, vmem, vmem, pl.BlockSpec(memory_space=pltpu.SMEM)],
        out_specs=vmem,
        scratch_shapes=[
            pltpu.VMEM((slots, queries, rows, cols), BF16),
            pltpu.VMEM((trains, slots, rows, cols), BF16),
            pltpu.VMEM((slots, trains, rows * cols), BF16),
            pltpu.VMEM((slots, 2, queries, rows * cols), BF16),
            pltpu.VMEM((slots, big, big), BF16),
            pltpu.VMEM((slots, big, 2 * cols), F32),
            pltpu.VMEM((2 * queries, trains), F32),
            pltpu.VMEM((4 * queries, 4 * queries), BF16),
            pltpu.VMEM((n, 4 * per, wide), BF16),
            pltpu.VMEM((n, 4 * per, wide), BF16),
            dma,
            dma((slots,)),
            dma((4,)),
            dma((slots,)),
            dma((slots,)),
            dma,
            dma,
        ],
        compiler_params=pltpu.CompilerParams(
            collective_id=0, has_side_effects=True, vmem_limit_bytes=50 * 1024 * 1024
        ),
    )(query_grads, train_grads, left_basis, right_basis, eigenvalues, block_rows)
    return scores * norm_scale


def solution(mesh):
    placed = (
        P(("mod", "pair"), None, None, None),
        P("pair", "mod", None, None),
        P("mod", None, None),
        P("mod", None, None),
        P("mod", None, None),
        P("mod"),
    )
    return jax.shard_map(
        functools.partial(on_device, mesh.shape["mod"]),
        mesh=mesh,
        in_specs=placed,
        out_specs=P("mod", "pair"),
        check_vma=False,
    )
```

time: 194 us -> 46.3 us (0.24)
  waiting for transfers between devices: 124 us -> 0 us
  Pallas kernels: 0 us -> 41.1 us
  matrix products: 27.6 us -> 0 us
  between operations: 13.5 us -> 0.01 us
  starting transfers between devices: 8.42 us -> 0 us
  local copies, waits for them, and re-layouts: 9.95 us -> 4.22 us
  loops' own time: 4.1 us -> 0 us
  other arithmetic: 4.27 us -> 0.61 us
    reduce_scatter x1 -> x0, waiting for transfers between devices: 99.6 us -> none  [on_device(): lax.psum_scatter(stacked.reshape(2 * per_source * lax.axis_size('mod'), -...]
    pallas_call x0 -> x1, Pallas kernels: none -> 41.1 us  [on_device(): pl.pallas_call(functools.partial(kernel, n), out_shape=jax.ShapeDtypeStru...]
    dot_general x6 -> x0, matrix products: 27.6 us -> none  [the longest x2 23.7 us: score_block(): lax.dot_general(left_rows, right_rows, (((1,), (1,)), ((), ())), preferre...]
    all_to_all x1 -> x0, waiting for transfers between devices: 24.4 us -> none  [on_device(): lax.all_to_all(query_grads, 'mod', split_axis=1, concat_axis=0, tiled=True)]
    all_to_all x1 -> x0, starting transfers between devices: 8.31 us -> none  [on_device(): lax.all_to_all(query_grads, 'mod', split_axis=1, concat_axis=0, tiled=True)]
    dynamic_slice x4 -> x0, local copies, waits for them, and re-layouts: 5 us -> none  [slot_turn(): live_rows = rows_all[slot_index]]
    another operation x5 -> x0, loops' own time: 4.1 us -> none  [the longest x1 2.62 us: precondition_slots(): lax.fori_loop(0, slot_count, slot_turn, jnp.zeros(grads.shape, jnp.bfloat...]
    unnamed x2 -> x10, local copies, waits for them, and re-layouts: 3.2 us -> 4.22 us
  transfers between devices with their start and end apart: 3 -> 0, of which waited for: 2 -> 0; matrix products, arithmetic and copies ran while one was open for 6% -> 0% of each run, Pallas kernels for 0% -> 0%
where the time goes in v1:
time: 46.3 us; the launch traced here: 45.9 us
  Pallas kernels  41.1 us (89%)
  local copies, waits for them, and re-layouts  4.22 us (9%)
  other arithmetic  0.61 us (1%)
    pallas_call x1, Pallas kernels, on_device(): pl.pallas_call(functools.partial(kernel, n), out_shape=jax.ShapeDtypeStru...  41.1 us
    unnamed x10, local copies, waits for them, and re-layouts  4.22 us

profile of v1, /device:TPU:0, one launch (start us, length us, event | category | flops | bytes accessed | tf_op | source)
XLA Modules:
  0.0 45.9 jit_solution(852886634941053360)
XLA Ops:
  0.0 0.0 copy-start
  0.0 1.2 %copy-done = bf16[4,64,16,128]{3,2,1,0:T(8,128)(2,1)S(1)} copy-done((bf16[4,64,16,128]{3,2,1,0:T(8,128)(2,1)S(1)}, bf16[4,64,16,128]{3,2,1,0:T(8,128)(2,1)}, u32[]{:S(2)}) %copy-start) | copy-done | bytes 1048600
  1.2 0.0 copy-start.1
  1.2 0.9 %copy-done.1 = bf16[4,128,128]{2,1,0:T(8,128)(2,1)S(1)} copy-done((bf16[4,128,128]{2,1,0:T(8,128)(2,1)S(1)}, bf16[4,128,128]{2,1,0:T(8,128)(2,1)}, u32[]{:S(2)}) %copy-start.1) | copy-done | bytes 131096
  2.1 0.0 copy-start.2
  2.1 0.7 %copy-done.2 = bf16[4,16,16]{2,1,0:T(8,128)(2,1)S(1)} copy-done((bf16[4,16,16]{2,1,0:T(8,128)(2,1)S(1)}, bf16[4,16,16]{2,1,0:T(8,128)(2,1)}, u32[]{:S(2)}) %copy-start.2) | copy-done | bytes 2072
  2.8 0.0 copy-start.3
  2.9 0.7 %copy-done.3 = bf16[4,16,128]{2,1,0:T(8,128)(2,1)S(1)} copy-done((bf16[4,16,128]{2,1,0:T(8,128)(2,1)S(1)}, bf16[4,16,128]{2,1,0:T(8,128)(2,1)}, u32[]{:S(2)}) %copy-start.3) | copy-done | bytes 16408
  3.6 0.0 copy-start.4
  3.6 0.7 %copy-done.4 = s32[4]{0:T(128)S(1)} copy-done((s32[4]{0:T(128)S(1)}, s32[4]{0:T(128)}, u32[]{:S(2)}) %copy-start.4) | copy-done | bytes 40
  4.2 41.1 %shard_map.64 = f32[8,512]{1,0:T(8,128)S(1)} custom-call(bf16[4,64,16,128]{3,2,1,0:T(8,128)(2,1)S(1)} %copy-done, bf16[512,4,16,128]{3,2,1,0:T(8,128)(2,1)} %t_ref.1, bf16[4,16,16]{2,1,0:T(8,128)(2,1)S(1)} %copy-done.2, bf16[4,128,128]{2,1,0:T(8,128)(2,1)S(1)} %copy-done.1, bf16[4,16,128]{2,1,0:T(8,128)(2,1)S(1)} %copy-done.3, s32[4]{0:T(128)S(1)} %copy-done.4), custom_call_target="tpu_custom_call" | custom-call | tf_op jit(solution)/shard_map/pallas_call | solution.py:209
  45.3 0.6 %broadcast_multiply_fusion = f32[8,512]{1,0:T(8,128)} fusion(f32[8,512]{1,0:T(8,128)S(1)} %shard_map.64), kind=kLoop, calls=%fused_computation | loop fusion | flops 4096 | bytes 32768 | tf_op jit(solution)/shard_map/mul | solution.py:237
Async XLA Ops:
  0.0 1.2 %copy-start = (bf16[4,64,16,128]{3,2,1,0:T(8,128)(2,1)S(1)}, bf16[4,64,16,128]{3,2,1,0:T(8,128)(2,1)}, u32[]{:S(2)}) copy-start(bf16[4,64,16,128]{3,2,1,0:T(8,128)(2,1)} %q_ref.1) | copy-start | bytes 3145732
  1.2 0.9 %copy-start.1 = (bf16[4,128,128]{2,1,0:T(8,128)(2,1)S(1)}, bf16[4,128,128]{2,1,0:T(8,128)(2,1)}, u32[]{:S(2)}) copy-start(bf16[4,128,128]{2,1,0:T(8,128)(2,1)} %right_ref.1) | copy-start | bytes 393220
  2.1 0.7 %copy-start.2 = (bf16[4,16,16]{2,1,0:T(8,128)(2,1)S(1)}, bf16[4,16,16]{2,1,0:T(8,128)(2,1)}, u32[]{:S(2)}) copy-start(bf16[4,16,16]{2,1,0:T(8,128)(2,1)} %left_ref.1) | copy-start | bytes 6148
  2.8 0.7 %copy-start.3 = (bf16[4,16,128]{2,1,0:T(8,128)(2,1)S(1)}, bf16[4,16,128]{2,1,0:T(8,128)(2,1)}, u32[]{:S(2)}) copy-start(bf16[4,16,128]{2,1,0:T(8,128)(2,1)} %eig_ref.1) | copy-start | bytes 49156
  3.6 0.7 %copy-start.4 = (s32[4]{0:T(128)S(1)}, s32[4]{0:T(128)}, u32[]{:S(2)}) copy-start(s32[4]{0:T(128)} %rows_ref.1) | copy-start | bytes 52

commit v2 on v1

--- a/solution.py
+++ b/solution.py
@@ -35,10 +35,10 @@
 
 def kernel(
     n,
-    q_ref, t_ref, left_ref, right_ref, eig_ref, rows_ref,
+    q_ref, t_ref, left_in, right_in, eig_in, rows_in,
     out_ref,
-    recv, tv, tr, sc, mixer, recip, acc, perm, msg, got,
-    send_sem, recv_sem, t_sem, pair_send, pair_recv, msg_send, msg_recv,
+    left_ref, right_ref, eig_ref, rows_ref, recv, tv, tr, sc, mixer, recip, acc, perm, msg, got,
+    small_sem, send_sem, recv_sem, t_sem, pair_send, pair_recv, msg_send, msg_recv,
 ):
     per, _, rows, cols = q_ref.shape
     trains, slots = t_ref.shape[0], t_ref.shape[1]
@@ -67,6 +67,14 @@
             t_ref.at[pl.ds(i * part, part)], tv.at[pl.ds(i * part, part)], t_sem.at[i]
         )
 
+    smalls = [
+        pltpu.make_async_copy(source, target, small_sem.at[i])
+        for i, (source, target) in enumerate(
+            [(left_in, left_ref), (eig_in, eig_ref), (rows_in, rows_ref), (right_in, right_ref)]
+        )
+    ]
+    for copy in smalls:
+        copy.start()
     for i in range(parts):
         train_copy(i).start()
 
@@ -90,6 +98,8 @@
             q_ref.at[:, me * slots + k], recv.at[k, pl.ds(me * per, per)], recv_sem.at[k]
         ).start()
 
+    for copy in smalls:
+        copy.wait()
     big = GROUP * rows
     pick_a = (iota((big, rows), 0) // GROUP == iota((big, rows), 1)).astype(BF16)
     pick_b = (lax.rem(iota((rows, big), 1), rows) == iota((rows, big), 0)).astype(BF16)
@@ -204,14 +214,18 @@
     wide = trains // 2
     norm_scale = 1.0 / math.sqrt(slot_total * rows * cols)
     vmem = pl.BlockSpec(memory_space=pltpu.VMEM)
-    parts = pl.BlockSpec(memory_space=pl.ANY)
+    parts = pl.BlockSpec(memory_space=pltpu.HBM)
     dma = pltpu.SemaphoreType.DMA
     scores = pl.pallas_call(
         functools.partial(kernel, n),
         out_shape=jax.ShapeDtypeStruct((2 * per, trains), F32),
-        in_specs=[parts, parts, vmem, vmem, vmem, pl.BlockSpec(memory_space=pltpu.SMEM)],
+        in_specs=[parts] * 6,
         out_specs=vmem,
         scratch_shapes=[
+            pltpu.VMEM(left_basis.shape, BF16),
+            pltpu.VMEM(right_basis.shape, BF16),
+            pltpu.VMEM(eigenvalues.shape, BF16),
+            pltpu.SMEM(block_rows.shape, jnp.int32),
             pltpu.VMEM((slots, queries, rows, cols), BF16),
             pltpu.VMEM((trains, slots, rows, cols), BF16),
             pltpu.VMEM((slots, trains, rows * cols), BF16),
@@ -222,6 +236,7 @@
             pltpu.VMEM((4 * queries, 4 * queries), BF16),
             pltpu.VMEM((n, 4 * per, wide), BF16),
             pltpu.VMEM((n, 4 * per, wide), BF16),
+            dma((4,)),
             dma,
             dma((slots,)),
             dma((4,)),
@@ -231,7 +246,7 @@
             dma,
         ],
         compiler_params=pltpu.CompilerParams(
-            collective_id=0, has_side_effects=True, vmem_limit_bytes=50 * 1024 * 1024
+            collective_id=0, has_side_effects=True, vmem_limit_bytes=58 * 1024 * 1024
         ),
     )(query_grads, train_grads, left_basis, right_basis, eigenvalues, block_rows)
     return scores * norm_scale

time: 46.3 us -> 42.8 us (0.924)
  local copies, waits for them, and re-layouts: 4.22 us -> 0 us
  other arithmetic: 0.61 us -> 1.33 us
    unnamed x10 -> x0, local copies, waits for them, and re-layouts: 4.22 us -> none
    mul x1, other arithmetic: 0.61 us -> 1.33 us  [on_device(): return scores * norm_scale]
where the time goes in v2:
time: 42.8 us; the launch traced here: 42.5 us
  Pallas kernels  41.2 us (96%)
  other arithmetic  1.33 us (3%)
    pallas_call x1, Pallas kernels, on_device(): pl.pallas_call(functools.partial(kernel, n), out_shape=jax.ShapeDtypeStru...  41.2 us
    mul x1, other arithmetic, on_device(): return scores * norm_scale  1.33 us

profile of v2, /device:TPU:0, one launch (start us, length us, event | category | flops | bytes accessed | tf_op | source)
XLA Modules:
  0.0 42.5 jit_solution(2159065961091776510)
XLA Ops:
  0.0 41.2 %shard_map.64 = f32[8,512]{1,0:T(8,128)} custom-call(bf16[4,64,16,128]{3,2,1,0:T(8,128)(2,1)} %q_ref.1, bf16[512,4,16,128]{3,2,1,0:T(8,128)(2,1)} %t_ref.1, bf16[4,16,16]{2,1,0:T(8,128)(2,1)} %left_in.1, bf16[4,128,128]{2,1,0:T(8,128)(2,1)} %right_in.1, bf16[4,16,128]{2,1,0:T(8,128)(2,1)} %eig_in.1, s32[4]{0:T(128)} %rows_in.1), custom_call_target="tpu_custom_call" | custom-call | tf_op jit(solution)/shard_map/pallas_call | solution.py:219
  41.2 1.3 %broadcast_multiply_fusion = f32[8,512]{1,0:T(8,128)} fusion(f32[8,512]{1,0:T(8,128)} %shard_map.64), kind=kLoop, calls=%fused_computation | loop fusion | flops 4096 | bytes 32768 | tf_op jit(solution)/shard_map/mul | solution.py:252
